TPU v7x, 256 devices: a whole 4x4x8 slice. The times are simulated.
256 devices in a mesh: noise: 8 (over z), row: 16 (over y, x), col: 2 (over core).
Axes of the slice: x: 4, y: 4, z: 8, core: 2. Of those that a mesh axis runs over, the one named last changes fastest.
Arguments:
- images: bfloat16 [256, 4, 6144], P('row', None, 'col'), may hold values from -40 to 40
- gain: float32 [6144], P('col'), may hold values from 0.3 to 3.5
- up_weight: bfloat16 [6144, 12288], P('col', 'row'), may hold values from -0.078125 to 0.078125
- down_weight: bfloat16 [12288, 6144], P('row', 'col'), may hold values from -0.0546875 to 0.0546875
- cotangent: bfloat16 [256, 16, 6144], P('row', 'noise', 'col'), may hold values from -6 to 6
- seeds: int32 [16], P('noise'), may hold values from 0 to 999999
- assign: int32 [16, 1], replicated, may hold values from 0 to 3, as said below
Outputs:
- saliency: float32 [256, 4, 6144], P('row', None, 'col')
Inputs may be any that keep to these rules, and one draw needn't show every extreme that they name: `assign`: every one of the 4 images is named by at least one copy.
All inputs are finite; a program needn't handle non-finite values.
Results may differ from a plain program's by a relative error of at most 0.0019.
Values may be sent and summed in bfloat16 or wider, within the bound.
A program may use at most 64 MiB of HBM per device.

v0:
```python
import math
import jax
import jax.numpy as jnp
from jax import lax
from jax.sharding import PartitionSpec as P

D = 6144
noise_scale = 0.6
gelu_coef = 0.044715
root_term = math.sqrt(2.0 / math.pi)


def mix_noise(seed_value, token_index, feature_index, width):
    linear = token_index[:, None] * width + feature_index[None, :]
    mixed = linear * 1664525 + seed_value * 1013904223
    mixed = mixed ^ mixed >> 13
    mixed = mixed * 1274126177
    mixed = mixed ^ mixed >> 16
    return ((mixed & 65535).astype(jnp.float32) - 32767.5) * (1.0 / 18918.0)


def gelu_slope(preact):
    inner = root_term * (preact + gelu_coef * preact * preact * preact)
    tanh_val = jnp.tanh(inner)
    return 0.5 * (1.0 + tanh_val) + 0.5 * preact * (1.0 - tanh_val * tanh_val) * root_term * (
        1.0 + 3.0 * gelu_coef * preact * preact
    )


def body(images, gain, up_weight, down_weight, cotangent, seeds, assign):
    tok_local = images.shape[0]
    image_count = images.shape[1]
    width_local = images.shape[2]
    planes = lax.axis_size("noise")
    rows = lax.axis_size("row")
    part = tok_local // planes
    col_index = lax.axis_index("col")
    row_index = lax.axis_index("row")
    noise_index = lax.axis_index("noise")
    all_seeds = lax.all_gather(seeds, "noise", tiled=True)
    slots = all_seeds.shape[0]
    own_cot = lax.all_to_all(cotangent, "noise", split_axis=0, concat_axis=1, tiled=True)
    own_images = lax.dynamic_slice_in_dim(images, noise_index * part, part)
    plane_images = lax.all_gather(own_images, "row", axis=0, tiled=True)
    plane_cot = lax.all_gather(own_cot, "row", axis=0, tiled=True)
    image_ids = jnp.arange(image_count, dtype=jnp.int32)
    onehot = (assign[:, 0][:, None] == image_ids[None, :]).astype(jnp.float32)
    counts = jnp.sum(onehot, axis=0)
    clean = jnp.einsum(
        "si,tid->tsd", onehot.astype(jnp.bfloat16), plane_images, preferred_element_type=jnp.float32
    )
    tokens = (
        jnp.arange(rows, dtype=jnp.int32)[:, None] * tok_local
        + noise_index * part
        + jnp.arange(part, dtype=jnp.int32)[None, :]
    ).reshape(-1)
    feature_index = col_index * width_local + jnp.arange(width_local, dtype=jnp.int32)
    noise_field = jax.vmap(
        lambda seed_value: mix_noise(seed_value, tokens, feature_index, D), out_axes=1
    )(all_seeds)
    noisy = clean + noise_scale * noise_field
    feat_mean = lax.psum(jnp.sum(noisy, axis=-1), "col") / D
    centred = noisy - feat_mean[..., None]
    feat_var = lax.psum(jnp.sum(centred * centred, axis=-1), "col") / D
    inv_std = lax.rsqrt(feat_var + 1e-06)
    normed = centred * inv_std[..., None]
    scaled = (normed * gain).astype(jnp.bfloat16)
    n = tokens.shape[0] * slots
    preact_part = jnp.dot(
        scaled.reshape(n, width_local), up_weight, preferred_element_type=jnp.float32
    )
    back_part = jnp.einsum(
        "td,hd->th",
        plane_cot.reshape(n, width_local),
        down_weight,
        preferred_element_type=jnp.float32,
    )
    ug_part = jnp.sum(gain[:, None] * up_weight.astype(jnp.float32), axis=0)
    preact, back_grad, ug = lax.psum((preact_part, back_part, ug_part), "col")
    hidden_grad = (back_grad * gelu_slope(preact)).astype(jnp.bfloat16)
    hg = hidden_grad.astype(jnp.float32)
    sums = jnp.stack([jnp.sum(hg * ug, axis=-1), jnp.sum(hg * preact, axis=-1)], axis=-1) / D
    sums = lax.psum_scatter(sums.reshape(-1, slots, 2), "row", scatter_dimension=0, tiled=True)
    weighted = jnp.einsum(
        "ts,si,tsh->tih",
        inv_std,
        onehot,
        hg.reshape(-1, slots, hg.shape[-1]),
        precision=lax.Precision.HIGHEST,
    ).astype(jnp.bfloat16)
    grad = jnp.einsum(
        "th,dh->td",
        weighted.reshape(-1, hg.shape[-1]),
        up_weight,
        preferred_element_type=jnp.float32,
    )
    grad = lax.psum_scatter(
        grad.reshape(-1, image_count, width_local), "row", scatter_dimension=0, tiled=True
    )
    own_normed = lax.dynamic_slice_in_dim(normed, row_index * part, part)
    own_inv = lax.dynamic_slice_in_dim(inv_std, row_index * part, part)
    rest = own_cot.astype(jnp.float32) - own_inv[..., None] * (
        sums[..., 0][..., None] + own_normed * sums[..., 1][..., None]
    )
    total = grad * gain + jnp.einsum("si,tsd->tid", onehot, rest, precision=lax.Precision.HIGHEST)
    total = total / counts[None, :, None]
    return lax.all_gather(total, "noise", axis=0, tiled=True)


def solution(mesh):
    placed = (
        P("row", None, "col"),
        P("col"),
        P("col", "row"),
        P("row", "col"),
        P("row", "noise", "col"),
        P("noise"),
        P(),
    )
    return jax.shard_map(
        body, mesh=mesh, in_specs=placed, out_specs=P("row", None, "col"), check_vma=False
    )
```

profile of v0, /device:TPU:2, one launch (start us, length us, event | category | flops | bytes accessed | tf_op | source)
XLA Modules:
  0.0 281.2 jit_solution(14509511110187522334)
XLA Ops:
  6.5 0.0 copy-start
  6.5 0.0 all-gather.2.cloned.1.call-start
  6.5 19.1 %all_to_all.18 = bf16[16,2,3072]{2,1,0:T(2,128)(2,1)S(1)} all-to-all(bf16[16,2,3072]{2,1,0:T(2,128)(2,1)} %param.11), channel_id=1, replica_groups=mesh['noise'=8,'row'=16,'col'=2] {'noise'}, dimensions={0} | all-to-all | bytes 393216 | tf_op jit(solution)/shard_map/all_to_all | solution.py:42
  25.6 0.1 copy.26
  25.7 0.8 all_to_all.16
  26.5 0.0 all-gather.2.cloned.1.call-update
  26.5 0.0 all-reduce.10.cloned.1.call-start
  26.6 0.1 add_multiply_fusion.1
  26.7 0.1 mul.175
  26.8 1.3 dynamic-slice
  28.8 0.9 dynamic-update-slice
  29.7 10.1 %all-reduce = s32[16]{0:T(128)S(1)} all-reduce(s32[16]{0:T(128)S(1)} %dynamic-update-slice), channel_id=1, replica_groups=mesh['noise'=8,'row'=16,'col'=2] {'noise'}, use_global_device_ids=true, to_apply=%add | all-reduce | flops 16 | bytes 128
  39.8 0.0 copy-done
  39.8 25.4 %all_gather.12 = bf16[32,4,3072]{2,1,0:T(4,128)(2,1)S(1)} all-gather(bf16[2,4,3072]{2,1,0:T(4,128)(2,1)S(1)} %constant_dynamic-slice_fusion.1), channel_id=1, replica_groups=mesh['noise'=8,'row'=16,'col'=2] {'row'}, dimensions={0}, use_global_device_ids=true | all-gather | bytes 835584 | tf_op jit(solution)/shard_map/all_gather | solution.py:44
  65.2 0.1 add_multiply_fusion
  65.3 5.3 %fusion.44 = (f32[32,16]{1,0:T(8,128)S(1)}, f32[32,16,3072]{2,1,0:T(8,128)}) fusion(s32[16]{0:T(128)S(1)} %broadcast_multiply_fusion.1, s32[32,3072]{1,0:T(8,128)S(1)} %add_multiply_fusion, bf16[32,4,3072]{2,1,0:T(4,128)(2,1)S(1)} %all_gather.12, s32[16]{0:T(128)} %bitcast.49), kind=kOutput, calls=%fused_computation.68 | convolution fusion | flops 31456960 | bytes 7473280 | tf_op jit(solution)/shard_map/si,tid->tsd/dot_general | solution.py:49
  70.7 3.5 %psum.35 = f32[32,16]{1,0:T(8,128)S(1)} all-reduce(f32[32,16]{1,0:T(8,128)S(1)} %get-tuple-element.18), channel_id=1, replica_groups=mesh['noise'=8,'row'=16,'col'=2] {'col'}, use_global_device_ids=true, to_apply=%region_1.0 | all-reduce | flops 512 | bytes 4096 | tf_op jit(solution)/shard_map/psum | solution.py:62
  74.1 3.5 %multiply_reduce_fusion.1 = f32[32,16]{1,0:T(8,128)S(1)} fusion(f32[32,16,3072]{2,1,0:T(8,128)} %get-tuple-element.19, f32[32,16]{1,0:T(8,128)S(1)} %broadcast_multiply_fusion), kind=kLoop, calls=%fused_computation.10 | loop fusion | flops 4718080 | bytes 6295552 | tf_op jit(solution)/shard_map/reduce_sum | solution.py:64
  77.7 0.0 copy-done.2
  77.7 0.0 slice-start
  77.7 3.4 %multiply_reduce_fusion = f32[768]{0:T(1024)S(1)} fusion(bf16[3072,768]{1,0:T(8,128)(2,1)} %param.9, f32[3072]{0:T(1024)S(1)} %copy-done.2), kind=kLoop, calls=%fused_computation.2 | loop fusion | flops 7077120 | bytes 4733952 | tf_op jit(solution)/shard_map/reduce_sum | solution.py:78
  81.1 3.6 %all-reduce.3 = (f32[32,16]{1,0:T(8,128)S(1)}, f32[768]{0:T(1024)S(1)}) all-reduce(f32[32,16]{1,0:T(8,128)S(1)} %multiply_reduce_fusion.1, f32[768]{0:T(1024)S(1)} %multiply_reduce_fusion), channel_id=1, replica_groups=mesh['noise'=8,'row'=16,'col'=2] {'col'}, use_global_device_ids=true, to_apply=%region_3.0 | all-reduce | flops 1280 | bytes 10240 | tf_op jit(solution)/shard_map/psum | solution.py:64
  84.7 0.0 slice-start.1
  84.7 7.3 %multiply_convert_fusion = (bf16[32,16,3072]{2,1,0:T(8,128)(2,1)S(1)}, f32[32,16,3072]{2,1,0:T(8,128)}) fusion(f32[3072]{0:T(1024)S(1)} %copy-done.2, f32[32,16]{1,0:T(8,128)S(1)} %get-tuple-element.17, f32[32,16,3072]{2,1,0:T(8,128)} %get-tuple-element.19, f32[32,16]{1,0:T(8,128)S(1)} %broadcast_multiply_fusion), kind=kLoop, calls=%fused_computation.9 | loop fusion | flops 6291456 | bytes 15745024 | tf_op jit(solution)/shard_map/convert_element_type | solution.py:67
  92.0 0.0 slice-done
  92.0 0.0 slice-done.1
  92.0 3.8 %fusion.46 = f32[512,768]{1,0:T(8,128)} fusion(bf16[512,3072]{1,0:T(8,128)(2,1)S(1)} %bitcast.46, bf16[3072,768]{1,0:T(8,128)(2,1)S(1)} %bitcast.44), kind=kOutput, calls=%fused_computation.70 | convolution fusion | flops 2415919104 | bytes 9437184 | tf_op jit(solution)/shard_map/dot_general | solution.py:69
  95.8 7.1 %fusion.45 = f32[512,768]{1,0:T(8,128)} fusion(bf16[512,3072]{1,0:T(8,128)(2,1)} %bitcast.53, bf16[768,3072]{1,0:T(8,128)(2,1)} %param.10), kind=kOutput, calls=%fused_computation.69 | convolution fusion | flops 2415919104 | bytes 9437184 | tf_op jit(solution)/shard_map/td,hd->th/dot_general | solution.py:72
  102.9 0.0 all-reduce.10.cloned.1.call-update
  102.9 0.2 all-reduce.8.cloned.1.call-start
  103.2 31.5 %all-reduce.10.cloned.1.call-done = (f32[512,768]{1,0:T(8,128)}, f32[512,768]{1,0:T(8,128)}) async-done(((f32[512,768]{1,0:T(8,128)}, f32[512,768]{1,0:T(8,128)}), (f32[512,768]{1,0:T(8,128)}, f32[512,768]{1,0:T(8,128)})) %all-reduce.10.cloned.1.call-update) | async-done | bytes 3145744 | tf_op jit(solution)/shard_map/psum | solution.py:79
  134.7 3.2 %fusion.10 = (f32[512]{0:T(512)S(1)}, f32[512]{0:T(512)S(1)}, bf16[512,768]{1,0:T(8,128)(2,1)S(1)}) fusion(f32[768]{0:T(1024)S(1)} %get-tuple-element.8, f32[512,768]{1,0:T(8,128)} %get-tuple-element.10, f32[512,768]{1,0:T(8,128)} %get-tuple-element.9), kind=kLoop, calls=%fused_computation.21 | loop fusion | flops 9436160 | bytes 3939328 | tf_op jit(solution)/shard_map/reduce_sum | solution.py:82
  137.9 0.5 convolution_convert_fusion
  138.3 0.0 copy-start.4
  138.4 0.0 copy-start.1
  138.4 4.0 %fusion.6 = f32[32,4,3072]{2,0,1:T(8,128)S(1)} fusion(bf16[3072,768]{1,0:T(8,128)(2,1)} %param.9, bf16[32,4,768]{2,1,0:T(4,128)(2,1)S(1)} %convolution_convert_fusion), kind=kOutput, calls=%fused_computation.12 | convolution fusion | flops 603979776 | bytes 6488064 | tf_op jit(solution)/shard_map/th,dh->td/dot_general | solution.py:91
  142.4 2.2 copy.20
  144.6 0.0 all-reduce.8.cloned.1.call-update
  144.7 0.6 dynamic-slice.1
  145.9 0.1 fusion.35
  146.1 0.1 stack.10
  146.1 0.1 stack.9
  146.2 69.6 %all-reduce.2 = f32[32,16,2]{1,0,2:T(8,128)S(1)} all-reduce(f32[32,16,2]{1,0,2:T(8,128)S(1)} %maximum_multiply_fusion), channel_id=3, replica_groups=mesh['noise'=8,'row'=16,'col'=2] {'row'}, use_global_device_ids=true, to_apply=%region_11.0.clone | all-reduce | flops 1024 | bytes 8192
  215.9 28.8 %all-reduce.8.cloned.1.call-done = f32[32,4,3072]{2,1,0:T(4,128)} async-done(((f32[32,4,3072]{2,1,0:T(4,128)}), f32[32,4,3072]{2,1,0:T(4,128)}) %all-reduce.8.cloned.1.call-update) | async-done | bytes 1572880
  244.7 0.0 copy-done.1
  244.7 1.4 fusion.9
  246.1 27.8 %all_gather.15 = f32[16,4,3072]{2,1,0:T(4,128)S(1)} all-gather(f32[2,4,3072]{2,1,0:T(4,128)S(1)} %fusion.9), channel_id=1, replica_groups=mesh['noise'=8,'row'=16,'col'=2] {'noise'}, dimensions={0}, use_global_device_ids=true | all-gather | bytes 884736 | tf_op jit(solution)/shard_map/all_gather | solution.py:107
  273.8 0.9 copy.32
  (17 shorter events, 0.1 us)
Async XLA Ops:
  6.5 33.3 %copy-start = (bf16[16,4,3072]{2,1,0:T(4,128)(2,1)S(1)}, bf16[16,4,3072]{2,1,0:T(4,128)(2,1)}, u32[]{:S(2)}) copy-start(bf16[16,4,3072]{2,1,0:T(4,128)(2,1)} %param.7) | copy-start | bytes 1179652
  6.5 89.3 %all-gather.2.cloned.1.call-start = ((), (), s32[]{:S(2)}) async-start(), calls=%async_computation.1 | async-start | bytes 3342336 | tf_op jit(solution)/shard_map/all_gather | solution.py:45
  26.5 108.2 %all-reduce.10.cloned.1.call-start = ((), (), s32[]{:S(2)}) async-start(), calls=%async_computation.3 | async-start | bytes 6291456 | tf_op jit(solution)/shard_map/psum | solution.py:79
  70.7 7.0 %copy-start.2 = (f32[3072]{0:T(1024)S(1)}, f32[3072]{0:T(1024)}, u32[]{:S(2)}) copy-start(f32[3072]{0:T(1024)} %param.8) | copy-start | bytes 36868
  77.7 14.3 %slice-start = ((s8[4718592]{0:T(1024)(128)(4,1)}), s8[524288]{0:T(1024)(128)(4,1)S(1)}, s32[]{:S(2)}) async-start(s8[4718592]{0:T(1024)(128)(4,1)} %bitcast.43), calls=%async_computation.4 | async-start | bytes 1048576
  84.7 7.3 %slice-start.1 = ((s8[4718592]{0:T(1024)(128)(4,1)}), s8[4194304]{0:T(1024)(128)(4,1)S(1)}, s32[]{:S(2)}) async-start(s8[4718592]{0:T(1024)(128)(4,1)} %bitcast.43), calls=%async_computation.5 | async-start | bytes 8388608
  95.8 7.3 %copy-start.3 = (s32[16,1]{0,1:T(1,128)S(1)}, s32[16,1]{0,1:T(1,128)}, u32[]{:S(2)}) copy-start(s32[16,1]{0,1:T(1,128)} %param.13) | copy-start | bytes 196
  102.9 141.7 %all-reduce.8.cloned.1.call-start = ((), (), s32[]{:S(2)}) async-start(), calls=%async_computation.2 | async-start | bytes 3145728
  138.3 6.3 %copy-start.4 = (u32[256]{0:T(256)S(1)}, u32[256]{0:T(256)}, u32[]{:S(2)}) copy-start(u32[256]{0:T(256)} %constant.75) | copy-start | bytes 3076
  138.4 106.3 %copy-start.1 = (bf16[2,16,3072]{2,1,0:T(8,128)(2,1)S(1)}, bf16[2,16,3072]{2,1,0:T(8,128)(2,1)}, u32[]{:S(2)}) copy-start(bf16[2,16,3072]{2,1,0:T(8,128)(2,1)} %all_to_all.16) | copy-start | bytes 589828
Sparse Core Ops, SparseCore 0:
  26.6 49.4 all-gather.1
  103.0 31.6 all-reduce.9
  144.8 99.8 all-reduce.7
where the time goes:
time: 282 us; the launch traced here: 281 us
  blocking collectives  159 us (56%)
  waiting for transfers between devices  60.4 us (21%)
  matrix products  22.1 us (8%)
  other arithmetic  17.7 us (6%)
  between operations  14.6 us (5%)
  local copies, waits for them, and re-layouts  7.19 us (3%)
    unnamed x2, blocking collectives  79.7 us
    psum x1, waiting for transfers between devices, body(): preact, back_grad, ug = lax.psum((preact_part, back_part, ug_part), 'col')  31.5 us
    unnamed x4, waiting for transfers between devices  28.8 us
    all_gather x1, blocking collectives, body(): return lax.all_gather(total, 'noise', axis=0, tiled=True)  27.8 us
    all_gather x1, blocking collectives, body(): plane_images = lax.all_gather(own_images, 'row', axis=0, tiled=True)  25.4 us
    all_to_all x1, blocking collectives, body(): lax.all_to_all(cotangent, 'noise', split_axis=0, concat_axis=1, tiled=True)  19.1 us
    convert_element_type x1, other arithmetic, body(): scaled = (normed * gain).astype(jnp.bfloat16)  7.28 us
    dot_general x1, matrix products, body(): jnp.einsum('td,hd->th', plane_cot.reshape(n, width_local), down_weight, p...  7.09 us
  transfers between devices with their start and end apart: 3, of which 2 were waited for; matrix products, arithmetic and copies ran while one was open for 10% of the time, Pallas kernels for 0%

commit v1 on v0

--- a/solution.py
+++ b/solution.py
@@ -8,6 +8,14 @@
 noise_scale = 0.6
 gelu_coef = 0.044715
 root_term = math.sqrt(2.0 / math.pi)
+
+
+def balance_samples(my_tile, which_axis):
+    long_array = jax.lax.all_to_all(
+        jnp.stack(jax.lax.psum(1, which_axis) * [my_tile]), which_axis, 0, 0
+    )
+    outer = jnp.concatenate(long_array, axis=0)
+    return outer
 
 
 def mix_noise(seed_value, token_index, feature_index, width):
@@ -104,7 +112,7 @@
     )
     total = grad * gain + jnp.einsum("si,tsd->tid", onehot, rest, precision=lax.Precision.HIGHEST)
     total = total / counts[None, :, None]
-    return lax.all_gather(total, "noise", axis=0, tiled=True)
+    return balance_samples(total, "noise")
 
 
 def solution(mesh):

time: 282 us -> 282 us (level)
    all_to_all x0 -> x1, blocking collectives: none -> 28.3 us  [balance_samples(): jax.lax.all_to_all(jnp.stack(jax.lax.psum(1, which_axis) * [my_tile]), wh...]
    all_gather x1 -> x0, blocking collectives: 27.8 us -> none  [body(): return lax.all_gather(total, 'noise', axis=0, tiled=True)]
where the time goes in v1:
time: 282 us
  blocking collectives  160 us (57%)
  waiting for transfers between devices  60.4 us (21%)
  matrix products  22.1 us (8%)
  other arithmetic  17.7 us (6%)
  between operations  14.6 us (5%)
  local copies, waits for them, and re-layouts  7.33 us (3%)
    unnamed x2, blocking collectives  79.7 us
    psum x1, waiting for transfers between devices, body(): preact, back_grad, ug = lax.psum((preact_part, back_part, ug_part), 'col')  31.5 us
    unnamed x4, waiting for transfers between devices  28.8 us
    all_to_all x1, blocking collectives, balance_samples(): jax.lax.all_to_all(jnp.stack(jax.lax.psum(1, which_axis) * [my_tile]), wh...  28.3 us
    all_gather x1, blocking collectives, body(): plane_images = lax.all_gather(own_images, 'row', axis=0, tiled=True)  25.4 us
    all_to_all x1, blocking collectives, body(): lax.all_to_all(cotangent, 'noise', split_axis=0, concat_axis=1, tiled=True)  19.1 us
    convert_element_type x1, other arithmetic, body(): scaled = (normed * gain).astype(jnp.bfloat16)  7.28 us
    dot_general x1, matrix products, body(): jnp.einsum('td,hd->th', plane_cot.reshape(n, width_local), down_weight, p...  7.09 us
  transfers between devices with their start and end apart: 3, of which 2 were waited for; matrix products, arithmetic and copies ran while one was open for 10% of the time, Pallas kernels for 0%

profile of v1, /device:TPU:2, one launch (start us, length us, event | category | flops | bytes accessed | tf_op | source)
XLA Modules:
  0.0 282.0 jit_solution(13066125752017076805)
XLA Ops:
  6.5 0.0 copy-start
  6.5 0.0 all-gather.2.cloned.1.call-start
  6.5 19.1 %all_to_all.23 = bf16[16,2,3072]{2,1,0:T(2,128)(2,1)S(1)} all-to-all(bf16[16,2,3072]{2,1,0:T(2,128)(2,1)} %param.11), channel_id=1, replica_groups=mesh['noise'=8,'row'=16,'col'=2] {'noise'}, dimensions={0} | all-to-all | bytes 393216 | tf_op jit(solution)/shard_map/all_to_all | solution.py:50
  25.6 0.1 copy.26
  25.7 0.8 all_to_all.19
  26.5 0.0 all-gather.2.cloned.1.call-update
  26.5 0.0 all-reduce.10.cloned.1.call-start
  26.6 0.1 add_multiply_fusion.1
  26.7 0.1 mul.175
  26.8 1.3 dynamic-slice
  28.8 0.9 dynamic-update-slice
  29.7 10.1 %all-reduce = s32[16]{0:T(128)S(1)} all-reduce(s32[16]{0:T(128)S(1)} %dynamic-update-slice), channel_id=1, replica_groups=mesh['noise'=8,'row'=16,'col'=2] {'noise'}, use_global_device_ids=true, to_apply=%add | all-reduce | flops 16 | bytes 128
  39.8 0.0 copy-done
  39.8 25.4 %all_gather.9 = bf16[32,4,3072]{2,1,0:T(4,128)(2,1)S(1)} all-gather(bf16[2,4,3072]{2,1,0:T(4,128)(2,1)S(1)} %constant_dynamic-slice_fusion.1), channel_id=1, replica_groups=mesh['noise'=8,'row'=16,'col'=2] {'row'}, dimensions={0}, use_global_device_ids=true | all-gather | bytes 835584 | tf_op jit(solution)/shard_map/all_gather | solution.py:52
  65.2 0.1 add_multiply_fusion
  65.3 5.3 %fusion.44 = (f32[32,16]{1,0:T(8,128)S(1)}, f32[32,16,3072]{2,1,0:T(8,128)}) fusion(s32[16]{0:T(128)S(1)} %broadcast_multiply_fusion.1, s32[32,3072]{1,0:T(8,128)S(1)} %add_multiply_fusion, bf16[32,4,3072]{2,1,0:T(4,128)(2,1)S(1)} %all_gather.9, s32[16]{0:T(128)} %bitcast.51), kind=kOutput, calls=%fused_computation.68 | convolution fusion | flops 31456960 | bytes 7473280 | tf_op jit(solution)/shard_map/si,tid->tsd/dot_general | solution.py:57
  70.7 3.5 %psum.35 = f32[32,16]{1,0:T(8,128)S(1)} all-reduce(f32[32,16]{1,0:T(8,128)S(1)} %get-tuple-element.18), channel_id=1, replica_groups=mesh['noise'=8,'row'=16,'col'=2] {'col'}, use_global_device_ids=true, to_apply=%region_1.0 | all-reduce | flops 512 | bytes 4096 | tf_op jit(solution)/shard_map/psum | solution.py:70
  74.1 3.5 %multiply_reduce_fusion.1 = f32[32,16]{1,0:T(8,128)S(1)} fusion(f32[32,16,3072]{2,1,0:T(8,128)} %get-tuple-element.19, f32[32,16]{1,0:T(8,128)S(1)} %broadcast_multiply_fusion), kind=kLoop, calls=%fused_computation.10 | loop fusion | flops 4718080 | bytes 6295552 | tf_op jit(solution)/shard_map/reduce_sum | solution.py:72
  77.7 0.0 copy-done.2
  77.7 0.0 slice-start
  77.7 3.4 %multiply_reduce_fusion = f32[768]{0:T(1024)S(1)} fusion(bf16[3072,768]{1,0:T(8,128)(2,1)} %param.9, f32[3072]{0:T(1024)S(1)} %copy-done.2), kind=kLoop, calls=%fused_computation.2 | loop fusion | flops 7077120 | bytes 4733952 | tf_op jit(solution)/shard_map/reduce_sum | solution.py:86
  81.1 3.6 %all-reduce.3 = (f32[32,16]{1,0:T(8,128)S(1)}, f32[768]{0:T(1024)S(1)}) all-reduce(f32[32,16]{1,0:T(8,128)S(1)} %multiply_reduce_fusion.1, f32[768]{0:T(1024)S(1)} %multiply_reduce_fusion), channel_id=1, replica_groups=mesh['noise'=8,'row'=16,'col'=2] {'col'}, use_global_device_ids=true, to_apply=%region_3.0 | all-reduce | flops 1280 | bytes 10240 | tf_op jit(solution)/shard_map/psum | solution.py:72
  84.7 0.0 slice-start.1
  84.7 7.3 %multiply_convert_fusion = (bf16[32,16,3072]{2,1,0:T(8,128)(2,1)S(1)}, f32[32,16,3072]{2,1,0:T(8,128)}) fusion(f32[3072]{0:T(1024)S(1)} %copy-done.2, f32[32,16]{1,0:T(8,128)S(1)} %get-tuple-element.17, f32[32,16,3072]{2,1,0:T(8,128)} %get-tuple-element.19, f32[32,16]{1,0:T(8,128)S(1)} %broadcast_multiply_fusion), kind=kLoop, calls=%fused_computation.9 | loop fusion | flops 6291456 | bytes 15745024 | tf_op jit(solution)/shard_map/convert_element_type | solution.py:75
  92.0 0.0 slice-done
  92.0 3.8 %fusion.46 = f32[512,768]{1,0:T(8,128)} fusion(bf16[512,3072]{1,0:T(8,128)(2,1)S(1)} %bitcast.48, bf16[3072,768]{1,0:T(8,128)(2,1)S(1)} %bitcast.45), kind=kOutput, calls=%fused_computation.70 | convolution fusion | flops 2415919104 | bytes 9437184 | tf_op jit(solution)/shard_map/dot_general | solution.py:77
  95.8 7.1 %fusion.45 = f32[512,768]{1,0:T(8,128)} fusion(bf16[512,3072]{1,0:T(8,128)(2,1)} %bitcast.55, bf16[768,3072]{1,0:T(8,128)(2,1)} %param.10), kind=kOutput, calls=%fused_computation.69 | convolution fusion | flops 2415919104 | bytes 9437184 | tf_op jit(solution)/shard_map/td,hd->th/dot_general | solution.py:80
  102.9 0.0 all-reduce.10.cloned.1.call-update
  102.9 0.2 all-reduce.8.cloned.1.call-start
  103.2 31.5 %all-reduce.10.cloned.1.call-done = (f32[512,768]{1,0:T(8,128)}, f32[512,768]{1,0:T(8,128)}) async-done(((f32[512,768]{1,0:T(8,128)}, f32[512,768]{1,0:T(8,128)}), (f32[512,768]{1,0:T(8,128)}, f32[512,768]{1,0:T(8,128)})) %all-reduce.10.cloned.1.call-update) | async-done | bytes 3145744 | tf_op jit(solution)/shard_map/psum | solution.py:87
  134.7 3.2 %fusion.10 = (f32[512]{0:T(512)S(1)}, f32[512]{0:T(512)S(1)}, bf16[512,768]{1,0:T(8,128)(2,1)S(1)}) fusion(f32[768]{0:T(1024)S(1)} %get-tuple-element.8, f32[512,768]{1,0:T(8,128)} %get-tuple-element.10, f32[512,768]{1,0:T(8,128)} %get-tuple-element.9), kind=kLoop, calls=%fused_computation.21 | loop fusion | flops 9436160 | bytes 3939328 | tf_op jit(solution)/shard_map/reduce_sum | solution.py:90
  137.9 0.5 convolution_convert_fusion
  138.3 0.0 copy-start.4
  138.4 0.0 copy-start.1
  138.4 4.0 %fusion.6 = f32[32,4,3072]{2,0,1:T(8,128)S(1)} fusion(bf16[3072,768]{1,0:T(8,128)(2,1)} %param.9, bf16[32,4,768]{2,1,0:T(4,128)(2,1)S(1)} %convolution_convert_fusion), kind=kOutput, calls=%fused_computation.12 | convolution fusion | flops 603979776 | bytes 6488064 | tf_op jit(solution)/shard_map/th,dh->td/dot_general | solution.py:99
  142.4 2.2 copy.20
  144.6 0.0 all-reduce.8.cloned.1.call-update
  144.7 0.6 dynamic-slice.1
  145.9 0.1 fusion.35
  146.1 0.1 stack.8
  146.1 0.1 stack.9
  146.2 69.6 %all-reduce.2 = f32[32,16,2]{1,0,2:T(8,128)S(1)} all-reduce(f32[32,16,2]{1,0,2:T(8,128)S(1)} %maximum_multiply_fusion), channel_id=3, replica_groups=mesh['noise'=8,'row'=16,'col'=2] {'row'}, use_global_device_ids=true, to_apply=%region_11.0.clone | all-reduce | flops 1024 | bytes 8192
  215.9 28.8 %all-reduce.8.cloned.1.call-done = f32[32,4,3072]{2,1,0:T(4,128)} async-done(((f32[32,4,3072]{2,1,0:T(4,128)}), f32[32,4,3072]{2,1,0:T(4,128)}) %all-reduce.8.cloned.1.call-update) | async-done | bytes 1572880
  244.7 0.0 copy-done.1
  244.7 1.4 fusion.9
  246.1 0.1 stack.11
  246.2 28.3 %all_to_all.24 = f32[8,2,4,3072]{3,2,1,0:T(4,128)S(1)} all-to-all(f32[8,2,4,3072]{3,2,1,0:T(4,128)S(1)} %stack.11), channel_id=1, replica_groups=mesh['noise'=8,'row'=16,'col'=2] {'noise'}, dimensions={0} | all-to-all | bytes 1572864 | tf_op jit(solution)/shard_map/all_to_all | solution.py:14
  274.6 0.9 copy.32
  (18 shorter events, 0.1 us)
Async XLA Ops:
  6.5 33.3 %copy-start = (bf16[16,4,3072]{2,1,0:T(4,128)(2,1)S(1)}, bf16[16,4,3072]{2,1,0:T(4,128)(2,1)}, u32[]{:S(2)}) copy-start(bf16[16,4,3072]{2,1,0:T(4,128)(2,1)} %param.7) | copy-start | bytes 1179652
  6.5 89.3 %all-gather.2.cloned.1.call-start = ((), (), s32[]{:S(2)}) async-start(), calls=%async_computation.2 | async-start | bytes 3342336 | tf_op jit(solution)/shard_map/all_gather | solution.py:53
  26.5 108.2 %all-reduce.10.cloned.1.call-start = ((), (), s32[]{:S(2)}) async-start(), calls=%async_computation.4 | async-start | bytes 6291456 | tf_op jit(solution)/shard_map/psum | solution.py:87
  70.7 7.0 %copy-start.2 = (f32[3072]{0:T(1024)S(1)}, f32[3072]{0:T(1024)}, u32[]{:S(2)}) copy-start(f32[3072]{0:T(1024)} %param.8) | copy-start | bytes 36868
  77.7 14.3 %slice-start = ((s8[4718592]{0:T(1024)(128)(4,1)}), s8[524288]{0:T(1024)(128)(4,1)S(1)}, s32[]{:S(2)}) async-start(s8[4718592]{0:T(1024)(128)(4,1)} %bitcast.44), calls=%async_computation.5 | async-start | bytes 1048576
  84.7 7.3 %slice-start.1 = ((s8[4718592]{0:T(1024)(128)(4,1)}), s8[4194304]{0:T(1024)(128)(4,1)S(1)}, s32[]{:S(2)}) async-start(s8[4718592]{0:T(1024)(128)(4,1)} %bitcast.44), calls=%async_computation.6 | async-start | bytes 8388608
  95.8 7.3 %copy-start.3 = (s32[16,1]{0,1:T(1,128)S(1)}, s32[16,1]{0,1:T(1,128)}, u32[]{:S(2)}) copy-start(s32[16,1]{0,1:T(1,128)} %param.13) | copy-start | bytes 196
  102.9 141.7 %all-reduce.8.cloned.1.call-start = ((), (), s32[]{:S(2)}) async-start(), calls=%async_computation.3 | async-start | bytes 3145728
  138.3 6.3 %copy-start.4 = (u32[256]{0:T(256)S(1)}, u32[256]{0:T(256)}, u32[]{:S(2)}) copy-start(u32[256]{0:T(256)} %constant.75) | copy-start | bytes 3076
  138.4 106.3 %copy-start.1 = (bf16[2,16,3072]{2,1,0:T(8,128)(2,1)S(1)}, bf16[2,16,3072]{2,1,0:T(8,128)(2,1)}, u32[]{:S(2)}) copy-start(bf16[2,16,3072]{2,1,0:T(8,128)(2,1)} %all_to_all.19) | copy-start | bytes 589828
Sparse Core Ops, SparseCore 0:
  26.6 49.4 all-gather.1
  103.0 31.6 all-reduce.9
  144.8 99.8 all-reduce.7
